TPU v7x, 256 devices: a whole 4x4x8 slice. The times are simulated.
256 devices in a mesh: req: 2 (over y_lo), ctx: 16 (over z, core), tp: 8 (over x, y_hi).
Axes of the slice: x: 4, y: 4 (y_hi: 2, y_lo: 2; y = y_hi * 2 + y_lo), z: 8, core: 2. Of those that a mesh axis runs over, the one named last changes fastest.
Arguments:
- queries: bfloat16 [1024, 16384], P(('req', 'ctx'), 'tp'), parts along dimension 0, may hold values from -200 to 200, as said below
- new_keys: bfloat16 [1024, 1024], P(('req', 'ctx'), 'tp'), parts along dimension 0, may hold values from -8 to 8, as said below
- fresh_values: bfloat16 [1024, 1024], P(('req', 'ctx'), 'tp'), parts along dimension 0, may hold values from -6 to 6
- history_keys: bfloat16 [65536, 1024], P(('req', 'ctx'), 'tp'), parts along dimension 0, may hold values from -6 to 6
- history_values: bfloat16 [65536, 1024], P(('req', 'ctx'), 'tp'), parts along dimension 0, may hold values from -6 to 6
- hist_lens: int32 [8], P('req'), parts along dimension 0, may hold values from 1 to 16384, 32768 in all
- new_lens: int32 [8], P('req'), parts along dimension 0, may hold values from 1 to 256, 512 in all
Outputs:
- attended: bfloat16 [1024, 16384], P(('req', 'ctx'), 'tp'), parts along dimension 0
There are 2 independent parts, one for each index of `req`. A program takes and returns all parts, laid end to end along the dimension named above; each array names one. Nothing has to cross between parts.
Inputs may be any that keep to these rules, and one draw needn't show every extreme that they name: Custom queries. `new_keys`: any values in the stated range. `hist_lens`: every request holds at least one history position; the largest holds exactly 16384. `new_lens`: every request holds at least one new token; the largest holds exactly 256.
All inputs are finite; a program needn't handle non-finite values.
Results may differ from a plain program's by a relative error of at most 0.018.
Values may be sent and summed in bfloat16 or wider, within the bound.
No kernel may reach another device: no remote copies, remote signals or barrier semaphores. Data moves between devices by JAX's collectives and lax.ppermute only.
A program may use at most 64 MiB of HBM per device.

v0:
```python
import functools
import math

import jax
import jax.numpy as jnp
from jax import lax
from jax.experimental import pallas as pl
from jax.experimental.pallas import tpu as pltpu
from jax.sharding import PartitionSpec as P

HEAD_SIZE = 128
REQS = 4
PIECES = 4
CHUNK = 128
STAT_ROWS = 16
LOG2_SCALE = math.log2(math.e) * HEAD_SIZE**-0.5
NEG = -3.0e38
FLOOR = -(2.0**100)


def ends_of(info, first):
    total = info[first]
    ends = [total]
    for r in range(1, REQS):
        total = total + info[first + r]
        ends.append(total)
    return ends


def request_of(position, ends):
    found = jnp.zeros_like(position)
    for end in ends[:-1]:
        found = found + (position >= end).astype(jnp.int32)
    return found


def pick(request, values):
    result = values[0]
    for r in range(1, len(values)):
        result = jnp.where(request == r, values[r], result)
    return result


def wide(column_block, width):
    if width <= 128:
        return column_block[:, :width]
    return jnp.concatenate([column_block] * (width // 128), axis=1)


def eye():
    rows = lax.broadcasted_iota(jnp.int32, (128, 128), 0)
    return rows == lax.broadcasted_iota(jnp.int32, (128, 128), 1)


def pack(top, total):
    high = total.astype(jnp.bfloat16).astype(jnp.float32)
    low = (total - high).astype(jnp.bfloat16).astype(jnp.float32)
    groups = top.shape[0] // 128
    diagonal = eye()
    at = lax.broadcasted_iota(jnp.int32, (STAT_ROWS, 128), 0)
    stats = jnp.zeros((STAT_ROWS, 128), jnp.float32)
    for kind, source in enumerate((top, high, low)):
        for g in range(groups):
            piece = source[g * 128 : (g + 1) * 128]
            row = jnp.sum(jnp.where(diagonal, piece, 0.0), axis=0, keepdims=True)
            stats = jnp.where(at == kind * groups + g, row, stats)
    return stats


def unpack(stats, rows):
    groups = rows // 128
    diagonal = eye()
    ones = jnp.ones((128, 128), jnp.bfloat16)

    def spread(i):
        row = jnp.broadcast_to(stats[i : i + 1].astype(jnp.float32), (128, 128))
        masked = jnp.where(diagonal, row, 0.0).astype(jnp.bfloat16)
        return jnp.dot(masked, ones, preferred_element_type=jnp.float32)

    top = jnp.concatenate([spread(g) for g in range(groups)], axis=0)
    total = jnp.concatenate([spread(groups + g) + spread(2 * groups + g) for g in range(groups)], axis=0)
    return top, total


def attend_kernel(shift, tokens, heads, chips, final, info_ref, q_ref, *refs):
    count_pieces = PIECES // 2
    if final:
        prior_ref, *refs = refs
        fresh_from, refs = refs[:PIECES], refs[PIECES:]
        piece_refs = fresh_from[count_pieces:]
    else:
        piece_refs, refs = refs[:count_pieces], refs[count_pieces:]
    out_ref, held_ref, new_ref, query_ref, score_ref, fresh_ref, top_ref, acc_ref, sems = refs
    rows = tokens * heads
    span = held_ref.shape[1] // 2
    half = span // 2
    chip, core = info_ref[2 * REQS], info_ref[2 * REQS + 1]
    hist_ends, new_ends = ends_of(info_ref, 0), ends_of(info_ref, REQS)
    hist_starts = [jnp.int32(0)] + hist_ends[:-1]

    owner = lax.rem(chip + shift * (2 * core - 1) + chips, chips)
    first_token = (owner * 2 + core) * tokens
    last_token = first_token + (tokens - 1)
    low_request = request_of(first_token, new_ends)
    high_request = request_of(last_token, new_ends)
    low, high = pick(low_request, hist_starts), pick(high_request, hist_ends)

    behind = 2 * lax.rem(chip + (chips - 1), chips)
    beyond = 2 * lax.rem(chip + 1, chips) + 1
    sources = [
        2 * chip + core,
        2 * chip + 1 - core,
        jnp.where(core == 0, behind, beyond),
        jnp.where(core == 0, beyond, behind),
    ]

    def seen(source):
        base = source * span
        first = (base < high) & (base + half > low)
        second = (base + half < high) & (base + span > low)
        last = source * tokens + (tokens - 1)
        fresh = (source * tokens <= last_token) & (request_of(last, new_ends) >= low_request)
        return first, second, fresh

    all_sources = sources
    any_fresh = functools.reduce(jnp.logical_or, [seen(source)[2] for source in all_sources])
    sources = all_sources[count_pieces:] if final else all_sources[:count_pieces]
    found = [seen(source) for source in sources]
    any_hist = functools.reduce(jnp.logical_or, [f | s for f, s, _ in found])
    if not final:
        any_fresh = jnp.bool_(False)

    def fetch(p):
        whole = piece_refs[p]
        return [
            pltpu.make_async_copy(whole.at[pl.ds(0, span)], held_ref.at[p, pl.ds(0, span)], sems.at[0, p]),
            pltpu.make_async_copy(
                whole.at[pl.ds(span + tokens, span)], held_ref.at[p, pl.ds(span, span)], sems.at[1, p]
            ),
        ]

    def fetch_new(p):
        whole = fresh_from[p]
        return [
            pltpu.make_async_copy(
                whole.at[pl.ds(span, tokens)], new_ref.at[0, pl.ds(p * tokens, tokens)], sems.at[2, p]
            ),
            pltpu.make_async_copy(
                whole.at[pl.ds(2 * span + tokens, tokens)], new_ref.at[1, pl.ds(p * tokens, tokens)], sems.at[3, p]
            ),
        ]

    if final:
        @pl.when(any_fresh)
        def _():
            for p in range(PIECES):
                for copy in fetch_new(p):
                    copy.start()

    for p in range(count_pieces):
        @pl.when(found[p][0] | found[p][1])
        def _(p=p):
            for copy in fetch(p):
                copy.start()

    @pl.when(jnp.logical_not(any_hist | any_fresh))
    def _():
        if final:
            out_ref[...] = prior_ref[...].astype(out_ref.dtype)
        else:
            out_ref[:rows] = jnp.zeros((rows, 128), out_ref.dtype)
            at = lax.broadcasted_iota(jnp.int32, (STAT_ROWS, 128), 0)
            out_ref[rows:] = jnp.where(at < rows // 128, FLOOR, 0.0).astype(out_ref.dtype)

    @pl.when(any_hist | any_fresh)
    def _():
        token = first_token + lax.broadcasted_iota(jnp.int32, (tokens, 1), 0)
        request = request_of(token, new_ends)
        row_low, row_high = pick(request, hist_starts), pick(request, hist_ends)
        for h in range(heads):
            query_ref[h * tokens : (h + 1) * tokens] = q_ref[:, h * HEAD_SIZE : (h + 1) * HEAD_SIZE]
        top_ref[...] = jnp.full((rows, 128), NEG, jnp.float32)
        acc_ref[...] = jnp.zeros((rows, 256), jnp.float32)

        def score(keys, mask, into_ref, column):
            count = keys.shape[0]
            for at in range(0, rows, CHUNK):
                part = pl.ds(at, CHUNK)
                scores = lax.dot_general(
                    query_ref[part], keys, (((1,), (1,)), ((), ())), preferred_element_type=jnp.float32
                )
                stacked = scores.reshape(CHUNK // tokens, tokens, count)
                scores = jnp.where(mask[None], stacked, NEG).reshape(CHUNK, count)
                into_ref[part, pl.ds(column, count)] = scores
                most = scores[:, :128]
                for j in range(128, count, 128):
                    most = jnp.maximum(most, scores[:, j : j + 128])
                top_ref[part] = jnp.maximum(top_ref[part], most)

        def weigh(values, from_ref, column):
            count = values.shape[0]
            both = jnp.concatenate([values, jnp.ones((count, 128), jnp.bfloat16)], axis=1)
            for at in range(0, rows, CHUNK):
                part = pl.ds(at, CHUNK)
                scores = from_ref[part, pl.ds(column, count)] * LOG2_SCALE
                weights = jnp.exp2(scores - wide(top_ref[part], count)).astype(jnp.bfloat16)
                acc_ref[part] += jnp.dot(weights, both, preferred_element_type=jnp.float32)

        def over_pieces(work):
            def piece(p, unused):
                source = pick(p, sources)
                first, second, _ = seen(source)
                column = pl.multiple_of(p * span, span)

                @pl.when(first & second)
                def _():
                    work(p, source, 0, span, column)

                @pl.when(first != second)
                def _():
                    skip = pl.multiple_of(jnp.where(first, 0, half), half)
                    work(p, source, skip, half, pl.multiple_of(column + skip, half))

                return unused

            lax.fori_loop(0, count_pieces, piece, 0)

        def score_piece(p, source, skip, count, column):
            position = source * span + skip + lax.broadcasted_iota(jnp.int32, (tokens, count), 1)
            mask = (position >= row_low) & (position < row_high)
            score(held_ref[p, pl.ds(skip, count)], mask, score_ref, column)

        def weigh_piece(p, source, skip, count, column):
            weigh(held_ref[p, pl.ds(span + skip, count)], score_ref, column)

        if final:
            @pl.when(any_fresh)
            def _():
                for p in range(PIECES):
                    for copy in fetch_new(p):
                        copy.wait()
                column = lax.broadcasted_iota(jnp.int32, (tokens, PIECES * tokens), 1)
                position = pick(lax.div(column, tokens), all_sources) * tokens + lax.rem(column, tokens)
                mask = (position <= token) & (request_of(position, new_ends) == request)
                score(new_ref[0], mask, fresh_ref, 0)

        for p in range(count_pieces):
            @pl.when(found[p][0] | found[p][1])
            def _(p=p):
                for copy in fetch(p):
                    copy.wait()

        over_pieces(score_piece)
        top = jnp.max(top_ref[...], axis=1, keepdims=True) * LOG2_SCALE
        top = jnp.maximum(top.astype(jnp.bfloat16).astype(jnp.float32), FLOOR)
        top_ref[...] = jnp.broadcast_to(top, (rows, 128))

        if final:
            @pl.when(any_fresh)
            def _():
                weigh(new_ref[1], fresh_ref, 0)

        over_pieces(weigh_piece)
        state = acc_ref[:, :128], top_ref[...], acc_ref[:, 128:]
        if final:
            state = merged([state, state_of(prior_ref, rows)])
        out_ref[:rows] = state[0].astype(out_ref.dtype)
        out_ref[rows:] = pack(state[1], state[2]).astype(out_ref.dtype)


def state_of(ref, rows):
    top, total = unpack(ref[rows:], rows)
    return ref[:rows].astype(jnp.float32), top, total


def merged(states):
    top = functools.reduce(jnp.maximum, [state[1] for state in states])
    numer = total = 0.0
    for part, part_top, part_total in states:
        scale = jnp.exp2(part_top - top)
        numer = numer + part * scale
        total = total + part_total * scale
    return numer, top, total


def finish_kernel(rows, tokens, heads, *refs):
    out_ref = refs[-1]
    numer, _, total = merged([state_of(ref, rows) for ref in refs[:-1]])
    result = (numer / total).astype(out_ref.dtype)
    for h in range(heads):
        out_ref[:, h * HEAD_SIZE : (h + 1) * HEAD_SIZE] = result[h * tokens : (h + 1) * tokens]


def attend_call(shift, tokens, heads, chips, info, block, prior, pieces, kind):
    rows = tokens * heads
    span = pieces[0].shape[0] // 2 - tokens
    final = prior is not None
    vmem = pl.BlockSpec(memory_space=pltpu.VMEM)
    smem = pl.BlockSpec(memory_space=pltpu.SMEM)
    anywhere = pl.BlockSpec(memory_space=pl.ANY)
    return pl.pallas_call(
        functools.partial(attend_kernel, shift, tokens, heads, chips, final),
        out_shape=jax.ShapeDtypeStruct((rows + STAT_ROWS, 128), kind),
        in_specs=[smem, vmem] + [vmem] * final + [anywhere] * len(pieces),
        out_specs=vmem,
        scratch_shapes=[
            pltpu.VMEM((PIECES // 2, 2 * span, 128), jnp.bfloat16),
            pltpu.VMEM((2, PIECES * tokens, 128), jnp.bfloat16),
            pltpu.VMEM((rows, 128), jnp.bfloat16),
            pltpu.VMEM((rows, PIECES // 2 * span), jnp.float32),
            pltpu.VMEM((rows, PIECES * tokens), jnp.float32),
            pltpu.VMEM((rows, 128), jnp.float32),
            pltpu.VMEM((rows, 256), jnp.float32),
            pltpu.SemaphoreType.DMA((4, PIECES)),
        ],
        compiler_params=pltpu.CompilerParams(vmem_limit_bytes=24 * 2**20),
        cost_estimate=pl.CostEstimate(flops=rows * 4096 * 128 * 4, bytes_accessed=2**21, transcendentals=0),
    )(info, block, *([prior] if final else []), *pieces)


def on_device(ctx, queries, new_keys, fresh_values, history_keys, history_values, hist_lens, new_lens):
    tokens, width = queries.shape
    span = history_keys.shape[0]
    heads = width // HEAD_SIZE
    rows = tokens * heads
    chips = ctx // 2
    me = lax.axis_index("ctx")
    info = jnp.concatenate([hist_lens, new_lens, jnp.stack([me // 2, me % 2]).astype(jnp.int32)])

    def swapped(array):
        return lax.ppermute(array, "ctx", [(i, i ^ 1) for i in range(ctx)])

    def moved(array, by):
        pairs = [(2 * z + c, 2 * ((z + by * (1 - 2 * c)) % chips) + c) for z in range(chips) for c in range(2)]
        return lax.ppermute(array, "ctx", pairs)

    reach = chips // 2
    shifts = [reach] + [s for by in range(2, reach, 2) for s in (by, -by)]
    guests = [moved(queries, shift) for shift in shifts]
    here = jnp.concatenate([history_keys, new_keys, history_values, fresh_values], axis=0)
    near = (here, swapped(here))
    waited = here
    passed = moved(waited, 1)
    vmem = pl.BlockSpec(memory_space=pltpu.VMEM)

    def attend(shift, block, prior, taken, kind):
        return attend_call(shift, tokens, heads, chips, info, block, prior, taken, kind)

    firsts = [attend(shift, block, None, near, jnp.float32) for shift, block in zip(shifts, guests, strict=True)]
    own = attend(0, queries, None, near, jnp.float32)
    passed, own, *firsts = lax.optimization_barrier((passed, own, *firsts))
    pieces = (*near, passed, swapped(passed))
    parts = [
        moved(attend(shift, block, first, pieces, jnp.bfloat16), -shift)
        for shift, block, first in zip(shifts, guests, firsts, strict=True)
    ]
    own = attend(0, queries, own, pieces, jnp.float32)
    return pl.pallas_call(
        functools.partial(finish_kernel, rows, tokens, heads),
        out_shape=jax.ShapeDtypeStruct((tokens, width), jnp.bfloat16),
        in_specs=[vmem] * (len(parts) + 1),
        out_specs=vmem,
        compiler_params=pltpu.CompilerParams(vmem_limit_bytes=16 * 2**20),
        cost_estimate=pl.CostEstimate(flops=rows * 2048, bytes_accessed=2**19, transcendentals=0),
    )(own, *parts)


def solution(mesh):
    split = P(("req", "ctx"), "tp")
    return jax.shard_map(
        functools.partial(on_device, mesh.shape["ctx"]),
        mesh=mesh,
        in_specs=(split,) * 5 + (P("req"),) * 2,
        out_specs=split,
        check_vma=False,
    )
```

profile of v0, /device:TPU:32, one launch (start us, length us, event | category | flops | bytes accessed | tf_op | source)
XLA Modules:
  0.0 63.2 jit_solution(581264316482908311)
XLA Ops:
  0.0 0.0 copy-start.1
  0.0 0.0 copy-start.2
  0.0 0.0 copy-start
  0.0 0.0 copy-start.3
  0.0 0.0 copy-start.4
  0.0 1.1 %constant_dynamic-update-slice_fusion.3 = bf16[4160,128]{1,0:T(8,128)(2,1)S(1)} fusion(bf16[2048,128]{1,0:T(8,128)(2,1)} %param.10), kind=kLoop, calls=%fused_computation.3 | loop fusion | bytes 1048576
  1.2 0.7 %constant_dynamic-update-slice_fusion.2 = bf16[4160,128]{1,0:T(8,128)(2,1)S(1)} fusion(bf16[4160,128]{1,0:T(8,128)(2,1)S(1)} %constant_dynamic-update-slice_fusion.3, bf16[32,128]{1,0:T(8,128)(2,1)} %param.8), kind=kLoop, calls=%fused_computation.2 | loop fusion | bytes 16384
  1.9 0.0 copy-done.1
  1.9 0.1 constant_dynamic-update-slice_fusion.1
  2.0 0.0 copy-done.2
  2.0 0.1 collective-permute-start.1
  2.1 2.0 %collective-permute-start = (bf16[4160,128]{1,0:T(8,128)(2,1)S(1)}, bf16[4160,128]{1,0:T(8,128)(2,1)S(1)}, u32[]{:S(2)}, u32[]{:S(2)}) collective-permute-start(bf16[4160,128]{1,0:T(8,128)(2,1)S(1)} %constant_dynamic-update-slice_fusion.refs_0_.refs_1_), channel_id=1, source_target_pairs={{0,16},{8,120},{16,32},{24,8},{32,48},{40,24},{48,64},{56,40},{64,... | collective-permute-start | bytes 3194888 | tf_op jit(solution)/shard_map/ppermute | solution.py:335
  4.1 0.0 copy-done
  4.1 4.5 %collective-permute-start.3 = (bf16[32,2048]{1,0:T(8,128)(2,1)S(1)}, bf16[32,2048]{1,0:T(8,128)(2,1)S(1)}, u32[]{:S(2)}, u32[]{:S(2)}) collective-permute-start(bf16[32,2048]{1,0:T(8,128)(2,1)S(1)} %copy-done), channel_id=1, source_target_pairs={{0,32},{8,104},{16,48},{24,120},{32,64},{40,8},{48,80},{56,24},{64... | collective-permute-start | bytes 393224 | tf_op jit(solution)/shard_map/ppermute | solution.py:335
  8.6 1.5 %collective-permute-start.2 = (bf16[32,2048]{1,0:T(8,128)(2,1)S(1)}, bf16[32,2048]{1,0:T(8,128)(2,1)}, u32[]{:S(2)}, u32[]{:S(2)}) collective-permute-start(bf16[32,2048]{1,0:T(8,128)(2,1)S(1)} %copy-done), channel_id=1, source_target_pairs={{0,64},{8,72},{16,80},{24,88},{32,96},{40,104},{48,112},{56,120},{... | collective-permute-start | bytes 393224 | tf_op jit(solution)/shard_map/ppermute | solution.py:335
  10.0 3.6 %collective-permute-start.4 = (bf16[32,2048]{1,0:T(8,128)(2,1)S(1)}, bf16[32,2048]{1,0:T(8,128)(2,1)}, u32[]{:S(2)}, u32[]{:S(2)}) collective-permute-start(bf16[32,2048]{1,0:T(8,128)(2,1)S(1)} %copy-done), channel_id=1, source_target_pairs={{0,96},{8,40},{16,112},{24,56},{32,0},{40,72},{48,16},{56,88},{64,... | collective-permute-start | bytes 393224 | tf_op jit(solution)/shard_map/ppermute | solution.py:335
  13.6 0.0 copy-done.3
  13.6 0.0 copy-done.4
  13.6 0.1 pad_add_fusion.info_ref
  13.7 0.0 collective-permute-done.1.refs_1_.refs_2_
  13.7 3.6 %shard_map.73.refs_0_ = f32[528,128]{1,0:T(8,128)S(1)} custom-call(s32[10]{0:T(128)S(1)} %pad_add_fusion.info_ref, bf16[32,2048]{1,0:T(8,128)(2,1)S(1)} %copy-done, bf16[4160,128]{1,0:T(8,128)(2,1)S(1)} %constant_dynamic-update-slice_fusion.refs_0_.refs_1_, bf16[4160,128]{1,0:T(8,128)(2,1)S(1)} %collective-permute-done.1.refs_1_.refs_2_), custom_call_target="tpu_custom_call" | custom-call | flops 1073741824 | bytes 2097152 | tf_op jit(solution)/shard_map/pallas_call | solution.py:301
  17.3 2.6 %collective-permute-done.4.q_ref = bf16[32,2048]{1,0:T(8,128)(2,1)} collective-permute-done((bf16[32,2048]{1,0:T(8,128)(2,1)S(1)}, bf16[32,2048]{1,0:T(8,128)(2,1)}, u32[]{:S(2)}, u32[]{:S(2)}) %collective-permute-start.4) | collective-permute-done | bytes 131104 | tf_op jit(solution)/shard_map/ppermute | solution.py:335
  19.9 1.1 %shard_map.76.refs_0_ = f32[528,128]{1,0:T(8,128)S(1)} custom-call(s32[10]{0:T(128)S(1)} %pad_add_fusion.info_ref, bf16[32,2048]{1,0:T(8,128)(2,1)} %collective-permute-done.4.q_ref, bf16[4160,128]{1,0:T(8,128)(2,1)S(1)} %constant_dynamic-update-slice_fusion.refs_0_.refs_1_, bf16[4160,128]{1,0:T(8,128)(2,1)S(1)} %collective-permute-done.1.refs_1_.refs_2_), custom_call_target="tpu_custom_call" | custom-call | flops 1073741824 | bytes 2097152 | tf_op jit(solution)/shard_map/pallas_call | solution.py:301
  21.1 6.5 %collective-permute-done.3.q_ref = bf16[32,2048]{1,0:T(8,128)(2,1)S(1)} collective-permute-done((bf16[32,2048]{1,0:T(8,128)(2,1)S(1)}, bf16[32,2048]{1,0:T(8,128)(2,1)S(1)}, u32[]{:S(2)}, u32[]{:S(2)}) %collective-permute-start.3) | collective-permute-done | bytes 131104 | tf_op jit(solution)/shard_map/ppermute | solution.py:335
  27.5 0.7 %shard_map.75.refs_0_ = f32[528,128]{1,0:T(8,128)S(1)} custom-call(s32[10]{0:T(128)S(1)} %pad_add_fusion.info_ref, bf16[32,2048]{1,0:T(8,128)(2,1)S(1)} %collective-permute-done.3.q_ref, bf16[4160,128]{1,0:T(8,128)(2,1)S(1)} %constant_dynamic-update-slice_fusion.refs_0_.refs_1_, bf16[4160,128]{1,0:T(8,128)(2,1)S(1)} %collective-permute-done.1.refs_1_.refs_2_), custom_call_target="tpu_custom_call" | custom-call | flops 1073741824 | bytes 2097152 | tf_op jit(solution)/shard_map/pallas_call | solution.py:301
  28.3 0.0 collective-permute-done.2.q_ref
  28.3 1.3 %shard_map.74.refs_0_ = f32[528,128]{1,0:T(8,128)S(1)} custom-call(s32[10]{0:T(128)S(1)} %pad_add_fusion.info_ref, bf16[32,2048]{1,0:T(8,128)(2,1)} %collective-permute-done.2.q_ref, bf16[4160,128]{1,0:T(8,128)(2,1)S(1)} %constant_dynamic-update-slice_fusion.refs_0_.refs_1_, bf16[4160,128]{1,0:T(8,128)(2,1)S(1)} %collective-permute-done.1.refs_1_.refs_2_), custom_call_target="tpu_custom_call" | custom-call | flops 1073741824 | bytes 2097152 | tf_op jit(solution)/shard_map/pallas_call | solution.py:301
  29.6 0.0 collective-permute-done.refs_3_
  29.6 4.1 %collective-permute-start.5 = (bf16[4160,128]{1,0:T(8,128)(2,1)S(1)}, bf16[4160,128]{1,0:T(8,128)(2,1)S(1)}, u32[]{:S(2)}, u32[]{:S(2)}) collective-permute-start(bf16[4160,128]{1,0:T(8,128)(2,1)S(1)} %collective-permute-done.refs_3_), channel_id=1, source_target_pairs={{0,8},{8,0},{16,24},{24,16},{32,40},{40,32},{48,56},{56,48},{64,72... | collective-permute-start | bytes 3194888 | tf_op jit(solution)/shard_map/ppermute | solution.py:331
  33.7 2.3 %collective-permute-done.5.refs_4_ = bf16[4160,128]{1,0:T(8,128)(2,1)S(1)} collective-permute-done((bf16[4160,128]{1,0:T(8,128)(2,1)S(1)}, bf16[4160,128]{1,0:T(8,128)(2,1)S(1)}, u32[]{:S(2)}, u32[]{:S(2)}) %collective-permute-start.5) | collective-permute-done | bytes 1064992 | tf_op jit(solution)/shard_map/ppermute | solution.py:331
  36.0 3.8 %shard_map.78 = bf16[528,128]{1,0:T(8,128)(2,1)S(1)} custom-call(s32[10]{0:T(128)S(1)} %pad_add_fusion.info_ref, bf16[32,2048]{1,0:T(8,128)(2,1)} %collective-permute-done.2.q_ref, f32[528,128]{1,0:T(8,128)S(1)} %shard_map.74.refs_0_, bf16[4160,128]{1,0:T(8,128)(2,1)S(1)} %constant_dynamic-update-slice_fusion.refs_0_.refs_1_, ...), custom_call_target="tpu_custom_call" | custom-call | flops 1073741824 | bytes 2097152 | tf_op jit(solution)/shard_map/pallas_call | solution.py:301
  39.9 2.5 %collective-permute-start.6 = (bf16[528,128]{1,0:T(8,128)(2,1)S(1)}, bf16[528,128]{1,0:T(8,128)(2,1)S(1)}, u32[]{:S(2)}, u32[]{:S(2)}) collective-permute-start(bf16[528,128]{1,0:T(8,128)(2,1)S(1)} %shard_map.78), channel_id=1, source_target_pairs={{0,64},{8,72},{16,80},{24,88},{32,96},{40,104},{48,112},{56,120},{... | collective-permute-start | bytes 405512 | tf_op jit(solution)/shard_map/ppermute | solution.py:335
  42.4 0.8 %shard_map.79 = bf16[528,128]{1,0:T(8,128)(2,1)S(1)} custom-call(s32[10]{0:T(128)S(1)} %pad_add_fusion.info_ref, bf16[32,2048]{1,0:T(8,128)(2,1)S(1)} %collective-permute-done.3.q_ref, f32[528,128]{1,0:T(8,128)S(1)} %shard_map.75.refs_0_, bf16[4160,128]{1,0:T(8,128)(2,1)S(1)} %constant_dynamic-update-slice_fusion.refs_0_.refs_1_, ...), custom_call_target="tpu_custom_call" | custom-call | flops 1073741824 | bytes 2097152 | tf_op jit(solution)/shard_map/pallas_call | solution.py:301
  43.2 7.4 %collective-permute-start.7 = (bf16[528,128]{1,0:T(8,128)(2,1)S(1)}, bf16[528,128]{1,0:T(8,128)(2,1)S(1)}, u32[]{:S(2)}, u32[]{:S(2)}) collective-permute-start(bf16[528,128]{1,0:T(8,128)(2,1)S(1)} %shard_map.79), channel_id=1, source_target_pairs={{0,96},{8,40},{16,112},{24,56},{32,0},{40,72},{48,16},{56,88},{64,... | collective-permute-start | bytes 405512 | tf_op jit(solution)/shard_map/ppermute | solution.py:335
  50.5 4.0 %shard_map.80 = bf16[528,128]{1,0:T(8,128)(2,1)S(1)} custom-call(s32[10]{0:T(128)S(1)} %pad_add_fusion.info_ref, bf16[32,2048]{1,0:T(8,128)(2,1)} %collective-permute-done.4.q_ref, f32[528,128]{1,0:T(8,128)S(1)} %shard_map.76.refs_0_, bf16[4160,128]{1,0:T(8,128)(2,1)S(1)} %constant_dynamic-update-slice_fusion.refs_0_.refs_1_, ...), custom_call_target="tpu_custom_call" | custom-call | flops 1073741824 | bytes 2097152 | tf_op jit(solution)/shard_map/pallas_call | solution.py:301
  54.6 0.1 collective-permute-start.8
  54.7 3.4 %shard_map.77.refs_0_ = f32[528,128]{1,0:T(8,128)S(1)} custom-call(s32[10]{0:T(128)S(1)} %pad_add_fusion.info_ref, bf16[32,2048]{1,0:T(8,128)(2,1)S(1)} %copy-done, f32[528,128]{1,0:T(8,128)S(1)} %shard_map.73.refs_0_, bf16[4160,128]{1,0:T(8,128)(2,1)S(1)} %constant_dynamic-update-slice_fusion.refs_0_.refs_1_, ...), custom_call_target="tpu_custom_call" | custom-call | flops 1073741824 | bytes 2097152 | tf_op jit(solution)/shard_map/pallas_call | solution.py:301
  58.1 0.0 collective-permute-done.6.refs_1_
  58.1 0.0 collective-permute-done.7.refs_2_
  58.1 3.6 %collective-permute-done.8.refs_3_ = bf16[528,128]{1,0:T(8,128)(2,1)S(1)} collective-permute-done((bf16[528,128]{1,0:T(8,128)(2,1)S(1)}, bf16[528,128]{1,0:T(8,128)(2,1)S(1)}, u32[]{:S(2)}, u32[]{:S(2)}) %collective-permute-start.8) | collective-permute-done | bytes 135200 | tf_op jit(solution)/shard_map/ppermute | solution.py:335
  61.8 1.4 %shard_map.81 = bf16[32,2048]{1,0:T(8,128)(2,1)} custom-call(f32[528,128]{1,0:T(8,128)S(1)} %shard_map.77.refs_0_, bf16[528,128]{1,0:T(8,128)(2,1)S(1)} %collective-permute-done.6.refs_1_, bf16[528,128]{1,0:T(8,128)(2,1)S(1)} %collective-permute-done.7.refs_2_, bf16[528,128]{1,0:T(8,128)(2,1)S(1)} %collective-permute-done.8.refs_3_), custom_call_target="tpu_custom_call" | custom-call | flops 1048576 | bytes 524288 | tf_op jit(solution)/shard_map/pallas_call | solution.py:358
  (1 shorter events, 0.0 us)
Async XLA Ops:
  0.0 1.9 %copy-start.1 = (bf16[2048,128]{1,0:T(8,128)(2,1)S(1)}, bf16[2048,128]{1,0:T(8,128)(2,1)}, u32[]{:S(2)}) copy-start(bf16[2048,128]{1,0:T(8,128)(2,1)} %param.11) | copy-start | bytes 1572868
  0.0 2.0 %copy-start.2 = (bf16[32,128]{1,0:T(8,128)(2,1)S(1)}, bf16[32,128]{1,0:T(8,128)(2,1)}, u32[]{:S(2)}) copy-start(bf16[32,128]{1,0:T(8,128)(2,1)} %param.9) | copy-start | bytes 24580
  0.0 4.1 %copy-start = (bf16[32,2048]{1,0:T(8,128)(2,1)S(1)}, bf16[32,2048]{1,0:T(8,128)(2,1)}, u32[]{:S(2)}) copy-start(bf16[32,2048]{1,0:T(8,128)(2,1)} %q_ref.3) | copy-start | bytes 393220
  0.0 13.6 %copy-start.3 = (s32[4]{0:T(128)S(1)}, s32[4]{0:T(128)}, u32[]{:S(2)}) copy-start(s32[4]{0:T(128)} %param.13) | copy-start | bytes 52
  0.0 13.6 %copy-start.4 = (s32[4]{0:T(128)S(1)}, s32[4]{0:T(128)}, u32[]{:S(2)}) copy-start(s32[4]{0:T(128)} %param.12) | copy-start | bytes 52
  2.0 11.7 %collective-permute-start.1 = (bf16[4160,128]{1,0:T(8,128)(2,1)S(1)}, bf16[4160,128]{1,0:T(8,128)(2,1)S(1)}, u32[]{:S(2)}, u32[]{:S(2)}) collective-permute-start(bf16[4160,128]{1,0:T(8,128)(2,1)S(1)} %constant_dynamic-update-slice_fusion.refs_0_.refs_1_), channel_id=1, source_target_pairs={{0,8},{8,0},{16,24},{24,16},{32,40},{40,32},{48,56},{56,48},{64,72... | collective-permute-start | bytes 3194888 | tf_op jit(solution)/shard_map/ppermute | solution.py:331
  2.1 27.5 %collective-permute-start = (bf16[4160,128]{1,0:T(8,128)(2,1)S(1)}, bf16[4160,128]{1,0:T(8,128)(2,1)S(1)}, u32[]{:S(2)}, u32[]{:S(2)}) collective-permute-start(bf16[4160,128]{1,0:T(8,128)(2,1)S(1)} %constant_dynamic-update-slice_fusion.refs_0_.refs_1_), channel_id=1, source_target_pairs={{0,16},{8,120},{16,32},{24,8},{32,48},{40,24},{48,64},{56,40},{64,... | collective-permute-start | bytes 3194888 | tf_op jit(solution)/shard_map/ppermute | solution.py:335
  4.1 23.5 %collective-permute-start.3 = (bf16[32,2048]{1,0:T(8,128)(2,1)S(1)}, bf16[32,2048]{1,0:T(8,128)(2,1)S(1)}, u32[]{:S(2)}, u32[]{:S(2)}) collective-permute-start(bf16[32,2048]{1,0:T(8,128)(2,1)S(1)} %copy-done), channel_id=1, source_target_pairs={{0,32},{8,104},{16,48},{24,120},{32,64},{40,8},{48,80},{56,24},{64... | collective-permute-start | bytes 393224 | tf_op jit(solution)/shard_map/ppermute | solution.py:335
  8.6 19.7 %collective-permute-start.2 = (bf16[32,2048]{1,0:T(8,128)(2,1)S(1)}, bf16[32,2048]{1,0:T(8,128)(2,1)}, u32[]{:S(2)}, u32[]{:S(2)}) collective-permute-start(bf16[32,2048]{1,0:T(8,128)(2,1)S(1)} %copy-done), channel_id=1, source_target_pairs={{0,64},{8,72},{16,80},{24,88},{32,96},{40,104},{48,112},{56,120},{... | collective-permute-start | bytes 393224 | tf_op jit(solution)/shard_map/ppermute | solution.py:335
  10.0 9.9 %collective-permute-start.4 = (bf16[32,2048]{1,0:T(8,128)(2,1)S(1)}, bf16[32,2048]{1,0:T(8,128)(2,1)}, u32[]{:S(2)}, u32[]{:S(2)}) collective-permute-start(bf16[32,2048]{1,0:T(8,128)(2,1)S(1)} %copy-done), channel_id=1, source_target_pairs={{0,96},{8,40},{16,112},{24,56},{32,0},{40,72},{48,16},{56,88},{64,... | collective-permute-start | bytes 393224 | tf_op jit(solution)/shard_map/ppermute | solution.py:335
  29.6 6.4 %collective-permute-start.5 = (bf16[4160,128]{1,0:T(8,128)(2,1)S(1)}, bf16[4160,128]{1,0:T(8,128)(2,1)S(1)}, u32[]{:S(2)}, u32[]{:S(2)}) collective-permute-start(bf16[4160,128]{1,0:T(8,128)(2,1)S(1)} %collective-permute-done.refs_3_), channel_id=1, source_target_pairs={{0,8},{8,0},{16,24},{24,16},{32,40},{40,32},{48,56},{56,48},{64,72... | collective-permute-start | bytes 3194888 | tf_op jit(solution)/shard_map/ppermute | solution.py:331
  39.9 18.2 %collective-permute-start.6 = (bf16[528,128]{1,0:T(8,128)(2,1)S(1)}, bf16[528,128]{1,0:T(8,128)(2,1)S(1)}, u32[]{:S(2)}, u32[]{:S(2)}) collective-permute-start(bf16[528,128]{1,0:T(8,128)(2,1)S(1)} %shard_map.78), channel_id=1, source_target_pairs={{0,64},{8,72},{16,80},{24,88},{32,96},{40,104},{48,112},{56,120},{... | collective-permute-start | bytes 405512 | tf_op jit(solution)/shard_map/ppermute | solution.py:335
  43.2 14.9 %collective-permute-start.7 = (bf16[528,128]{1,0:T(8,128)(2,1)S(1)}, bf16[528,128]{1,0:T(8,128)(2,1)S(1)}, u32[]{:S(2)}, u32[]{:S(2)}) collective-permute-start(bf16[528,128]{1,0:T(8,128)(2,1)S(1)} %shard_map.79), channel_id=1, source_target_pairs={{0,96},{8,40},{16,112},{24,56},{32,0},{40,72},{48,16},{56,88},{64,... | collective-permute-start | bytes 405512 | tf_op jit(solution)/shard_map/ppermute | solution.py:335
  54.6 7.2 %collective-permute-start.8 = (bf16[528,128]{1,0:T(8,128)(2,1)S(1)}, bf16[528,128]{1,0:T(8,128)(2,1)S(1)}, u32[]{:S(2)}, u32[]{:S(2)}) collective-permute-start(bf16[528,128]{1,0:T(8,128)(2,1)S(1)} %shard_map.80), channel_id=1, source_target_pairs={{0,32},{8,104},{16,48},{24,120},{32,64},{40,8},{48,80},{56,24},{64... | collective-permute-start | bytes 405512 | tf_op jit(solution)/shard_map/ppermute | solution.py:335
where the time goes:
time: 62.8 us; the launch traced here: 63.2 us
  starting transfers between devices  25.7 us (41%)
  Pallas kernels  20.2 us (32%)
  waiting for transfers between devices  15.1 us (24%)
  local copies, waits for them, and re-layouts  1.94 us (3%)
    ppermute x7, starting transfers between devices, moved(): return lax.ppermute(array, 'ctx', pairs)  21.5 us
    pallas_call x8, Pallas kernels, attend_call(): pl.pallas_call(functools.partial(attend_kernel, shift, tokens, heads, chi...  18.8 us
    ppermute x7, waiting for transfers between devices, moved(): return lax.ppermute(array, 'ctx', pairs)  12.7 us
    ppermute x2, starting transfers between devices, swapped(): return lax.ppermute(array, 'ctx', [(i, i ^ 1) for i in range(ctx)])  4.22 us
    ppermute x2, waiting for transfers between devices, swapped(): return lax.ppermute(array, 'ctx', [(i, i ^ 1) for i in range(ctx)])  2.31 us
    unnamed x13, local copies, waits for them, and re-layouts  1.93 us
    pallas_call x1, Pallas kernels, on_device(): pl.pallas_call(functools.partial(finish_kernel, rows, tokens, heads), out...  1.41 us
  transfers between devices with their start and end apart: 9, of which 4 were waited for; matrix products, arithmetic and copies ran while one was open for 0% of the time, Pallas kernels for 24%

commit v1 on v0

--- a/solution.py
+++ b/solution.py
@@ -82,10 +82,11 @@
     return top, total
 
 
-def attend_kernel(shift, tokens, heads, chips, final, info_ref, q_ref, *refs):
+def attend_kernel(shift, tokens, heads, chips, priors, info_ref, q_ref, *refs):
     count_pieces = PIECES // 2
+    final = priors > 0
     if final:
-        prior_ref, *refs = refs
+        prior_refs, refs = refs[:priors], refs[priors:]
         fresh_from, refs = refs[:PIECES], refs[PIECES:]
         piece_refs = fresh_from[count_pieces:]
     else:
@@ -130,14 +131,12 @@
     if not final:
         any_fresh = jnp.bool_(False)
 
-    def fetch(p):
-        whole = piece_refs[p]
-        return [
-            pltpu.make_async_copy(whole.at[pl.ds(0, span)], held_ref.at[p, pl.ds(0, span)], sems.at[0, p]),
-            pltpu.make_async_copy(
-                whole.at[pl.ds(span + tokens, span)], held_ref.at[p, pl.ds(span, span)], sems.at[1, p]
-            ),
-        ]
+    def fetch(kind, p, source_ref):
+        return pltpu.make_async_copy(
+            source_ref.at[pl.ds(kind * (span + tokens), span)],
+            held_ref.at[p, pl.ds(kind * span, span)],
+            sems.at[kind, p],
+        )
 
     def fetch_new(p):
         whole = fresh_from[p]
@@ -157,16 +156,22 @@
                 for copy in fetch_new(p):
                     copy.start()
 
-    for p in range(count_pieces):
-        @pl.when(found[p][0] | found[p][1])
-        def _(p=p):
-            for copy in fetch(p):
-                copy.start()
+    for kind in range(2):
+        for p in range(count_pieces):
+            @pl.when(found[p][0] | found[p][1])
+            def _(kind=kind, p=p):
+                fetch(kind, p, piece_refs[p]).start()
+
+    def write(state):
+        out_ref[:rows] = state[0].astype(out_ref.dtype)
+        out_ref[rows:] = pack(state[1], state[2]).astype(out_ref.dtype)
 
     @pl.when(jnp.logical_not(any_hist | any_fresh))
     def _():
-        if final:
-            out_ref[...] = prior_ref[...].astype(out_ref.dtype)
+        if priors == 1:
+            out_ref[...] = prior_refs[0][...].astype(out_ref.dtype)
+        elif final:
+            write(merged([state_of(ref, rows) for ref in prior_refs]))
         else:
             out_ref[:rows] = jnp.zeros((rows, 128), out_ref.dtype)
             at = lax.broadcasted_iota(jnp.int32, (STAT_ROWS, 128), 0)
@@ -206,11 +211,15 @@
                 weights = jnp.exp2(scores - wide(top_ref[part], count)).astype(jnp.bfloat16)
                 acc_ref[part] += jnp.dot(weights, both, preferred_element_type=jnp.float32)
 
-        def over_pieces(work):
+        def over_pieces(work, kind):
             def piece(p, unused):
                 source = pick(p, sources)
                 first, second, _ = seen(source)
                 column = pl.multiple_of(p * span, span)
+
+                @pl.when(first | second)
+                def _():
+                    fetch(kind, p, piece_refs[0]).wait()
 
                 @pl.when(first & second)
                 def _():
@@ -244,13 +253,7 @@
                 mask = (position <= token) & (request_of(position, new_ends) == request)
                 score(new_ref[0], mask, fresh_ref, 0)
 
-        for p in range(count_pieces):
-            @pl.when(found[p][0] | found[p][1])
-            def _(p=p):
-                for copy in fetch(p):
-                    copy.wait()
-
-        over_pieces(score_piece)
+        over_pieces(score_piece, 0)
         top = jnp.max(top_ref[...], axis=1, keepdims=True) * LOG2_SCALE
         top = jnp.maximum(top.astype(jnp.bfloat16).astype(jnp.float32), FLOOR)
         top_ref[...] = jnp.broadcast_to(top, (rows, 128))
@@ -260,12 +263,11 @@
             def _():
                 weigh(new_ref[1], fresh_ref, 0)
 
-        over_pieces(weigh_piece)
+        over_pieces(weigh_piece, 1)
         state = acc_ref[:, :128], top_ref[...], acc_ref[:, 128:]
         if final:
-            state = merged([state, state_of(prior_ref, rows)])
-        out_ref[:rows] = state[0].astype(out_ref.dtype)
-        out_ref[rows:] = pack(state[1], state[2]).astype(out_ref.dtype)
+            state = merged([state] + [state_of(ref, rows) for ref in prior_refs])
+        write(state)
 
 
 def state_of(ref, rows):
@@ -291,17 +293,17 @@
         out_ref[:, h * HEAD_SIZE : (h + 1) * HEAD_SIZE] = result[h * tokens : (h + 1) * tokens]
 
 
-def attend_call(shift, tokens, heads, chips, info, block, prior, pieces, kind):
+def attend_call(shift, tokens, heads, chips, info, block, priors, pieces, kind):
     rows = tokens * heads
     span = pieces[0].shape[0] // 2 - tokens
-    final = prior is not None
+    count = len(priors)
     vmem = pl.BlockSpec(memory_space=pltpu.VMEM)
     smem = pl.BlockSpec(memory_space=pltpu.SMEM)
     anywhere = pl.BlockSpec(memory_space=pl.ANY)
     return pl.pallas_call(
-        functools.partial(attend_kernel, shift, tokens, heads, chips, final),
+        functools.partial(attend_kernel, shift, tokens, heads, chips, count),
         out_shape=jax.ShapeDtypeStruct((rows + STAT_ROWS, 128), kind),
-        in_specs=[smem, vmem] + [vmem] * final + [anywhere] * len(pieces),
+        in_specs=[smem, vmem] + [vmem] * count + [anywhere] * len(pieces),
         out_specs=vmem,
         scratch_shapes=[
             pltpu.VMEM((PIECES // 2, 2 * span, 128), jnp.bfloat16),
@@ -315,7 +317,7 @@
         ],
         compiler_params=pltpu.CompilerParams(vmem_limit_bytes=24 * 2**20),
         cost_estimate=pl.CostEstimate(flops=rows * 4096 * 128 * 4, bytes_accessed=2**21, transcendentals=0),
-    )(info, block, *([prior] if final else []), *pieces)
+    )(info, block, *priors, *pieces)
 
 
 def on_device(ctx, queries, new_keys, fresh_values, history_keys, history_values, hist_lens, new_lens):
@@ -334,27 +336,29 @@
         pairs = [(2 * z + c, 2 * ((z + by * (1 - 2 * c)) % chips) + c) for z in range(chips) for c in range(2)]
         return lax.ppermute(array, "ctx", pairs)
 
-    reach = chips // 2
-    shifts = [reach] + [s for by in range(2, reach, 2) for s in (by, -by)]
-    guests = [moved(queries, shift) for shift in shifts]
     here = jnp.concatenate([history_keys, new_keys, history_values, fresh_values], axis=0)
+    ahead = moved(queries, 2)
+    back = moved(queries, -2)
+    here, ahead = lax.optimization_barrier((here, ahead))
+    passed = moved(here, 1)
+    far = moved(ahead, 2)
     near = (here, swapped(here))
-    waited = here
-    passed = moved(waited, 1)
     vmem = pl.BlockSpec(memory_space=pltpu.VMEM)
 
-    def attend(shift, block, prior, taken, kind):
-        return attend_call(shift, tokens, heads, chips, info, block, prior, taken, kind)
-
-    firsts = [attend(shift, block, None, near, jnp.float32) for shift, block in zip(shifts, guests, strict=True)]
-    own = attend(0, queries, None, near, jnp.float32)
-    passed, own, *firsts = lax.optimization_barrier((passed, own, *firsts))
+    def attend(shift, block, priors, taken, kind):
+        return attend_call(shift, tokens, heads, chips, info, block, priors, taken, kind)
+
+    f32, bf16 = jnp.float32, jnp.bfloat16
+    visits = ((0, queries), (2, ahead), (-2, back))
+    own, ahead_part, back_part = [attend(shift, block, (), near, f32) for shift, block in visits]
+    passed, own, ahead_part, back_part, far = lax.optimization_barrier((passed, own, ahead_part, back_part, far))
     pieces = (*near, passed, swapped(passed))
-    parts = [
-        moved(attend(shift, block, first, pieces, jnp.bfloat16), -shift)
-        for shift, block, first in zip(shifts, guests, firsts, strict=True)
-    ]
-    own = attend(0, queries, own, pieces, jnp.float32)
+    far_part = attend(4, far, (), near, f32)
+    far_part = moved(attend(4, far, (far_part,), pieces, bf16), -2)
+    back_part = moved(attend(-2, back, (back_part,), pieces, bf16), 2)
+    ahead_part = moved(attend(2, ahead, (ahead_part, far_part), pieces, bf16), -2)
+    own = attend(0, queries, (own,), pieces, f32)
+    parts = (ahead_part, back_part)
     return pl.pallas_call(
         functools.partial(finish_kernel, rows, tokens, heads),
         out_shape=jax.ShapeDtypeStruct((tokens, width), jnp.bfloat16),

time: 62.8 us -> 58.4 us (0.930)
  the two profiles are of different devices: /device:TPU:32 before, /device:TPU:2 now
where the time goes in v1:
time: 58.4 us; the launch traced here: 57.8 us
  waiting for transfers between devices  21.1 us (36%)
  Pallas kernels  17.9 us (31%)
  starting transfers between devices  17.3 us (30%)
  other arithmetic  1.38 us (2%)
    ppermute x7, waiting for transfers between devices, moved(): return lax.ppermute(array, 'ctx', pairs)  19.2 us
    ppermute x7, starting transfers between devices, moved(): return lax.ppermute(array, 'ctx', pairs)  17.3 us
    pallas_call x8, Pallas kernels, attend_call(): pl.pallas_call(functools.partial(attend_kernel, shift, tokens, heads, chi...  16.6 us
    ppermute x2, waiting for transfers between devices, swapped(): return lax.ppermute(array, 'ctx', [(i, i ^ 1) for i in range(ctx)])  1.93 us
    concatenate x1, other arithmetic, on_device(): jnp.concatenate([history_keys, new_keys, history_values, fresh_values], a...  1.3 us
    pallas_call x1, Pallas kernels, on_device(): pl.pallas_call(functools.partial(finish_kernel, rows, tokens, heads), out...  1.25 us
  transfers between devices with their start and end apart: 9, of which 6 were waited for; matrix products, arithmetic and copies ran while one was open for 2% of the time, Pallas kernels for 27%

profile of v1, /device:TPU:2, one launch (start us, length us, event | category | flops | bytes accessed | tf_op | source)
XLA Modules:
  0.0 57.8 jit_solution(5467938318577803093)
XLA Ops:
  0.0 0.0 copy-start
  0.0 0.0 copy-start.2
  0.0 0.0 copy-start.1
  0.0 3.3 %collective-permute-start = (bf16[32,2048]{1,0:T(8,128)(2,1)}, bf16[32,2048]{1,0:T(8,128)(2,1)S(1)}, u32[]{:S(2)}, u32[]{:S(2)}) collective-permute-start(bf16[32,2048]{1,0:T(8,128)(2,1)} %q_ref.3), channel_id=1, source_target_pairs={{0,32},{8,104},{16,48},{24,120},{32,64},{40,8},{48,80},{56,24},{64... | collective-permute-start | bytes 393224 | tf_op jit(solution)/shard_map/ppermute | solution.py:337
  3.4 1.3 %pad_maximum_fusion.refs_0_.refs_1_.refs_2_ = bf16[4160,128]{1,0:T(8,128)(2,1)S(1)} fusion(bf16[32,128]{1,0:T(8,128)(2,1)} %param.9, bf16[2048,128]{1,0:T(8,128)(2,1)} %param.11, bf16[32,128]{1,0:T(8,128)(2,1)} %param.8, bf16[2048,128]{1,0:T(8,128)(2,1)} %param.10), kind=kLoop, calls=%fused_computation | loop fusion | flops 4259840 | bytes 2129920 | tf_op jit(solution)/shard_map/concatenate | solution.py:339
  4.7 5.0 %collective-permute-done.q_ref = bf16[32,2048]{1,0:T(8,128)(2,1)S(1)} collective-permute-done((bf16[32,2048]{1,0:T(8,128)(2,1)}, bf16[32,2048]{1,0:T(8,128)(2,1)S(1)}, u32[]{:S(2)}, u32[]{:S(2)}) %collective-permute-start) | collective-permute-done | bytes 131104 | tf_op jit(solution)/shard_map/ppermute | solution.py:337
  9.6 0.0 collective-permute-start.2
  9.6 2.3 %collective-permute-start.1 = (bf16[4160,128]{1,0:T(8,128)(2,1)S(1)}, bf16[4160,128]{1,0:T(8,128)(2,1)S(1)}, u32[]{:S(2)}, u32[]{:S(2)}) collective-permute-start(bf16[4160,128]{1,0:T(8,128)(2,1)S(1)} %pad_maximum_fusion.refs_0_.refs_1_.refs_2_), channel_id=1, source_target_pairs={{0,16},{8,120},{16,32},{24,8},{32,48},{40,24},{48,64},{56,40},{64,... | collective-permute-start | bytes 3194888 | tf_op jit(solution)/shard_map/ppermute | solution.py:337
  12.0 0.0 copy-done
  12.0 2.9 %collective-permute-start.3 = (bf16[32,2048]{1,0:T(8,128)(2,1)S(1)}, bf16[32,2048]{1,0:T(8,128)(2,1)}, u32[]{:S(2)}, u32[]{:S(2)}) collective-permute-start(bf16[32,2048]{1,0:T(8,128)(2,1)S(1)} %copy-done), channel_id=1, source_target_pairs={{0,96},{8,40},{16,112},{24,56},{32,0},{40,72},{48,16},{56,88},{64,... | collective-permute-start | bytes 393224 | tf_op jit(solution)/shard_map/ppermute | solution.py:337
  14.9 0.0 copy-done.2
  14.9 0.0 copy-done.1
  14.9 0.1 pad_add_fusion.info_ref
  15.0 0.0 collective-permute-start.4
  15.0 0.0 collective-permute-done.2.refs_1_.refs_2_.refs_3_
  15.0 0.7 %shard_map.74.refs_0_ = f32[528,128]{1,0:T(8,128)S(1)} custom-call(s32[10]{0:T(128)S(1)} %pad_add_fusion.info_ref, bf16[32,2048]{1,0:T(8,128)(2,1)S(1)} %collective-permute-done.q_ref, bf16[4160,128]{1,0:T(8,128)(2,1)S(1)} %pad_maximum_fusion.refs_0_.refs_1_.refs_2_, bf16[4160,128]{1,0:T(8,128)(2,1)S(1)} %collective-permute-done.2.refs_1_.refs_2_.refs_3_), custom_call_target="tpu_custom_call" | custom-call | flops 1073741824 | bytes 2097152 | tf_op jit(solution)/shard_map/pallas_call | solution.py:303
  15.8 4.2 %shard_map.73.refs_0_ = f32[528,128]{1,0:T(8,128)S(1)} custom-call(s32[10]{0:T(128)S(1)} %pad_add_fusion.info_ref, bf16[32,2048]{1,0:T(8,128)(2,1)S(1)} %copy-done, bf16[4160,128]{1,0:T(8,128)(2,1)S(1)} %pad_maximum_fusion.refs_0_.refs_1_.refs_2_, bf16[4160,128]{1,0:T(8,128)(2,1)S(1)} %collective-permute-done.2.refs_1_.refs_2_.refs_3_), custom_call_target="tpu_custom_call" | custom-call | flops 1073741824 | bytes 2097152 | tf_op jit(solution)/shard_map/pallas_call | solution.py:303
  20.0 0.4 collective-permute-done.3.q_ref
  20.4 1.1 %shard_map.75.refs_0_ = f32[528,128]{1,0:T(8,128)S(1)} custom-call(s32[10]{0:T(128)S(1)} %pad_add_fusion.info_ref, bf16[32,2048]{1,0:T(8,128)(2,1)} %collective-permute-done.3.q_ref, bf16[4160,128]{1,0:T(8,128)(2,1)S(1)} %pad_maximum_fusion.refs_0_.refs_1_.refs_2_, bf16[4160,128]{1,0:T(8,128)(2,1)S(1)} %collective-permute-done.2.refs_1_.refs_2_.refs_3_), custom_call_target="tpu_custom_call" | custom-call | flops 1073741824 | bytes 2097152 | tf_op jit(solution)/shard_map/pallas_call | solution.py:303
  21.5 12.0 %collective-permute-done.4.q_ref = bf16[32,2048]{1,0:T(8,128)(2,1)S(1)} collective-permute-done((bf16[32,2048]{1,0:T(8,128)(2,1)S(1)}, bf16[32,2048]{1,0:T(8,128)(2,1)S(1)}, u32[]{:S(2)}, u32[]{:S(2)}) %collective-permute-start.4) | collective-permute-done | bytes 131104 | tf_op jit(solution)/shard_map/ppermute | solution.py:337
  33.5 0.0 collective-permute-done.1.refs_3_.refs_4_
  33.5 0.0 collective-permute-start.5
  33.5 0.7 %shard_map.77.refs_0_ = f32[528,128]{1,0:T(8,128)S(1)} custom-call(s32[10]{0:T(128)S(1)} %pad_add_fusion.info_ref, bf16[32,2048]{1,0:T(8,128)(2,1)S(1)} %collective-permute-done.4.q_ref, bf16[4160,128]{1,0:T(8,128)(2,1)S(1)} %pad_maximum_fusion.refs_0_.refs_1_.refs_2_, bf16[4160,128]{1,0:T(8,128)(2,1)S(1)} %collective-permute-done.2.refs_1_.refs_2_.refs_3_), custom_call_target="tpu_custom_call" | custom-call | flops 1073741824 | bytes 2097152 | tf_op jit(solution)/shard_map/pallas_call | solution.py:303
  34.2 1.9 %collective-permute-done.5.refs_4_.refs_5_ = bf16[4160,128]{1,0:T(8,128)(2,1)S(1)} collective-permute-done((bf16[4160,128]{1,0:T(8,128)(2,1)S(1)}, bf16[4160,128]{1,0:T(8,128)(2,1)S(1)}, u32[]{:S(2)}, u32[]{:S(2)}) %collective-permute-start.5) | collective-permute-done | bytes 1064992 | tf_op jit(solution)/shard_map/ppermute | solution.py:333
  36.1 0.8 %shard_map.78 = bf16[528,128]{1,0:T(8,128)(2,1)S(1)} custom-call(s32[10]{0:T(128)S(1)} %pad_add_fusion.info_ref, bf16[32,2048]{1,0:T(8,128)(2,1)S(1)} %collective-permute-done.4.q_ref, f32[528,128]{1,0:T(8,128)S(1)} %shard_map.77.refs_0_, bf16[4160,128]{1,0:T(8,128)(2,1)S(1)} %pad_maximum_fusion.refs_0_.refs_1_.refs_2_, ...), custom_call_target="tpu_custom_call" | custom-call | flops 1073741824 | bytes 2097152 | tf_op jit(solution)/shard_map/pallas_call | solution.py:303
  36.9 3.9 %collective-permute-start.6 = (bf16[528,128]{1,0:T(8,128)(2,1)S(1)}, bf16[528,128]{1,0:T(8,128)(2,1)S(1)}, u32[]{:S(2)}, u32[]{:S(2)}) collective-permute-start(bf16[528,128]{1,0:T(8,128)(2,1)S(1)} %shard_map.78), channel_id=1, source_target_pairs={{0,96},{8,40},{16,112},{24,56},{32,0},{40,72},{48,16},{56,88},{64,... | collective-permute-start | bytes 405512 | tf_op jit(solution)/shard_map/ppermute | solution.py:337
  40.8 2.3 %shard_map.80 = bf16[528,128]{1,0:T(8,128)(2,1)S(1)} custom-call(s32[10]{0:T(128)S(1)} %pad_add_fusion.info_ref, bf16[32,2048]{1,0:T(8,128)(2,1)} %collective-permute-done.3.q_ref, f32[528,128]{1,0:T(8,128)S(1)} %shard_map.75.refs_0_, bf16[4160,128]{1,0:T(8,128)(2,1)S(1)} %pad_maximum_fusion.refs_0_.refs_1_.refs_2_, ...), custom_call_target="tpu_custom_call" | custom-call | flops 1073741824 | bytes 2097152 | tf_op jit(solution)/shard_map/pallas_call | solution.py:303
  43.1 0.1 collective-permute-start.8
  43.2 1.6 %collective-permute-done.6.refs_1_ = bf16[528,128]{1,0:T(8,128)(2,1)S(1)} collective-permute-done((bf16[528,128]{1,0:T(8,128)(2,1)S(1)}, bf16[528,128]{1,0:T(8,128)(2,1)S(1)}, u32[]{:S(2)}, u32[]{:S(2)}) %collective-permute-start.6) | collective-permute-done | bytes 135200 | tf_op jit(solution)/shard_map/ppermute | solution.py:337
  44.8 3.3 %shard_map.79 = bf16[528,128]{1,0:T(8,128)(2,1)S(1)} custom-call(s32[10]{0:T(128)S(1)} %pad_add_fusion.info_ref, bf16[32,2048]{1,0:T(8,128)(2,1)S(1)} %collective-permute-done.q_ref, f32[528,128]{1,0:T(8,128)S(1)} %shard_map.74.refs_0_, bf16[528,128]{1,0:T(8,128)(2,1)S(1)} %collective-permute-done.6.refs_1_, ...), custom_call_target="tpu_custom_call" | custom-call | flops 1073741824 | bytes 2097152 | tf_op jit(solution)/shard_map/pallas_call | solution.py:303
  48.1 4.7 %collective-permute-start.7 = (bf16[528,128]{1,0:T(8,128)(2,1)S(1)}, bf16[528,128]{1,0:T(8,128)(2,1)S(1)}, u32[]{:S(2)}, u32[]{:S(2)}) collective-permute-start(bf16[528,128]{1,0:T(8,128)(2,1)S(1)} %shard_map.79), channel_id=1, source_target_pairs={{0,96},{8,40},{16,112},{24,56},{32,0},{40,72},{48,16},{56,88},{64,... | collective-permute-start | bytes 405512 | tf_op jit(solution)/shard_map/ppermute | solution.py:337
  52.9 3.4 %shard_map.76.refs_0_ = f32[528,128]{1,0:T(8,128)S(1)} custom-call(s32[10]{0:T(128)S(1)} %pad_add_fusion.info_ref, bf16[32,2048]{1,0:T(8,128)(2,1)S(1)} %copy-done, f32[528,128]{1,0:T(8,128)S(1)} %shard_map.73.refs_0_, bf16[4160,128]{1,0:T(8,128)(2,1)S(1)} %pad_maximum_fusion.refs_0_.refs_1_.refs_2_, ...), custom_call_target="tpu_custom_call" | custom-call | flops 1073741824 | bytes 2097152 | tf_op jit(solution)/shard_map/pallas_call | solution.py:303
  56.3 0.0 collective-permute-done.8.refs_2_
  56.3 0.2 collective-permute-done.7.refs_1_
  56.5 1.3 %shard_map.81 = bf16[32,2048]{1,0:T(8,128)(2,1)} custom-call(f32[528,128]{1,0:T(8,128)S(1)} %shard_map.76.refs_0_, bf16[528,128]{1,0:T(8,128)(2,1)S(1)} %collective-permute-done.7.refs_1_, bf16[528,128]{1,0:T(8,128)(2,1)S(1)} %collective-permute-done.8.refs_2_), custom_call_target="tpu_custom_call" | custom-call | flops 1048576 | bytes 524288 | tf_op jit(solution)/shard_map/pallas_call | solution.py:362
Async XLA Ops:
  0.0 12.0 %copy-start = (bf16[32,2048]{1,0:T(8,128)(2,1)S(1)}, bf16[32,2048]{1,0:T(8,128)(2,1)}, u32[]{:S(2)}) copy-start(bf16[32,2048]{1,0:T(8,128)(2,1)} %q_ref.3) | copy-start | bytes 393220
  0.0 14.9 %copy-start.2 = (s32[4]{0:T(128)S(1)}, s32[4]{0:T(128)}, u32[]{:S(2)}) copy-start(s32[4]{0:T(128)} %param.12) | copy-start | bytes 52
  0.0 14.9 %copy-start.1 = (s32[4]{0:T(128)S(1)}, s32[4]{0:T(128)}, u32[]{:S(2)}) copy-start(s32[4]{0:T(128)} %param.13) | copy-start | bytes 52
  0.0 9.6 %collective-permute-start = (bf16[32,2048]{1,0:T(8,128)(2,1)}, bf16[32,2048]{1,0:T(8,128)(2,1)S(1)}, u32[]{:S(2)}, u32[]{:S(2)}) collective-permute-start(bf16[32,2048]{1,0:T(8,128)(2,1)} %q_ref.3), channel_id=1, source_target_pairs={{0,32},{8,104},{16,48},{24,120},{32,64},{40,8},{48,80},{56,24},{64... | collective-permute-start | bytes 393224 | tf_op jit(solution)/shard_map/ppermute | solution.py:337
  9.6 5.4 %collective-permute-start.2 = (bf16[4160,128]{1,0:T(8,128)(2,1)S(1)}, bf16[4160,128]{1,0:T(8,128)(2,1)S(1)}, u32[]{:S(2)}, u32[]{:S(2)}) collective-permute-start(bf16[4160,128]{1,0:T(8,128)(2,1)S(1)} %pad_maximum_fusion.refs_0_.refs_1_.refs_2_), channel_id=1, source_target_pairs={{0,8},{8,0},{16,24},{24,16},{32,40},{40,32},{48,56},{56,48},{64,72... | collective-permute-start | bytes 3194888 | tf_op jit(solution)/shard_map/ppermute | solution.py:333
  9.6 23.8 %collective-permute-start.1 = (bf16[4160,128]{1,0:T(8,128)(2,1)S(1)}, bf16[4160,128]{1,0:T(8,128)(2,1)S(1)}, u32[]{:S(2)}, u32[]{:S(2)}) collective-permute-start(bf16[4160,128]{1,0:T(8,128)(2,1)S(1)} %pad_maximum_fusion.refs_0_.refs_1_.refs_2_), channel_id=1, source_target_pairs={{0,16},{8,120},{16,32},{24,8},{32,48},{40,24},{48,64},{56,40},{64,... | collective-permute-start | bytes 3194888 | tf_op jit(solution)/shard_map/ppermute | solution.py:337
  12.0 8.4 %collective-permute-start.3 = (bf16[32,2048]{1,0:T(8,128)(2,1)S(1)}, bf16[32,2048]{1,0:T(8,128)(2,1)}, u32[]{:S(2)}, u32[]{:S(2)}) collective-permute-start(bf16[32,2048]{1,0:T(8,128)(2,1)S(1)} %copy-done), channel_id=1, source_target_pairs={{0,96},{8,40},{16,112},{24,56},{32,0},{40,72},{48,16},{56,88},{64,... | collective-permute-start | bytes 393224 | tf_op jit(solution)/shard_map/ppermute | solution.py:337
  15.0 18.5 %collective-permute-start.4 = (bf16[32,2048]{1,0:T(8,128)(2,1)S(1)}, bf16[32,2048]{1,0:T(8,128)(2,1)S(1)}, u32[]{:S(2)}, u32[]{:S(2)}) collective-permute-start(bf16[32,2048]{1,0:T(8,128)(2,1)S(1)} %collective-permute-done.q_ref), channel_id=1, source_target_pairs={{0,32},{8,104},{16,48},{24,120},{32,64},{40,8},{48,80},{56,24},{64... | collective-permute-start | bytes 393224 | tf_op jit(solution)/shard_map/ppermute | solution.py:337
  33.5 2.7 %collective-permute-start.5 = (bf16[4160,128]{1,0:T(8,128)(2,1)S(1)}, bf16[4160,128]{1,0:T(8,128)(2,1)S(1)}, u32[]{:S(2)}, u32[]{:S(2)}) collective-permute-start(bf16[4160,128]{1,0:T(8,128)(2,1)S(1)} %collective-permute-done.1.refs_3_.refs_4_), channel_id=1, source_target_pairs={{0,8},{8,0},{16,24},{24,16},{32,40},{40,32},{48,56},{56,48},{64,72... | collective-permute-start | bytes 3194888 | tf_op jit(solution)/shard_map/ppermute | solution.py:333
  36.9 7.9 %collective-permute-start.6 = (bf16[528,128]{1,0:T(8,128)(2,1)S(1)}, bf16[528,128]{1,0:T(8,128)(2,1)S(1)}, u32[]{:S(2)}, u32[]{:S(2)}) collective-permute-start(bf16[528,128]{1,0:T(8,128)(2,1)S(1)} %shard_map.78), channel_id=1, source_target_pairs={{0,96},{8,40},{16,112},{24,56},{32,0},{40,72},{48,16},{56,88},{64,... | collective-permute-start | bytes 405512 | tf_op jit(solution)/shard_map/ppermute | solution.py:337
  43.1 13.2 %collective-permute-start.8 = (bf16[528,128]{1,0:T(8,128)(2,1)S(1)}, bf16[528,128]{1,0:T(8,128)(2,1)S(1)}, u32[]{:S(2)}, u32[]{:S(2)}) collective-permute-start(bf16[528,128]{1,0:T(8,128)(2,1)S(1)} %shard_map.80), channel_id=1, source_target_pairs={{0,32},{8,104},{16,48},{24,120},{32,64},{40,8},{48,80},{56,24},{64... | collective-permute-start | bytes 405512 | tf_op jit(solution)/shard_map/ppermute | solution.py:337
  48.1 8.4 %collective-permute-start.7 = (bf16[528,128]{1,0:T(8,128)(2,1)S(1)}, bf16[528,128]{1,0:T(8,128)(2,1)S(1)}, u32[]{:S(2)}, u32[]{:S(2)}) collective-permute-start(bf16[528,128]{1,0:T(8,128)(2,1)S(1)} %shard_map.79), channel_id=1, source_target_pairs={{0,96},{8,40},{16,112},{24,56},{32,0},{40,72},{48,16},{56,88},{64,... | collective-permute-start | bytes 405512 | tf_op jit(solution)/shard_map/ppermute | solution.py:337

commit v2 on v1

--- a/solution.py
+++ b/solution.py
@@ -291,6 +291,24 @@
     result = (numer / total).astype(out_ref.dtype)
     for h in range(heads):
         out_ref[:, h * HEAD_SIZE : (h + 1) * HEAD_SIZE] = result[h * tokens : (h + 1) * tokens]
+
+
+def merge_kernel(rows, own_ref, got_ref, out_ref):
+    numer, top, total = merged([state_of(own_ref, rows), state_of(got_ref, rows)])
+    out_ref[:rows] = numer.astype(out_ref.dtype)
+    out_ref[rows:] = pack(top, total).astype(out_ref.dtype)
+
+
+def merge_call(rows, own, got):
+    vmem = pl.BlockSpec(memory_space=pltpu.VMEM)
+    return pl.pallas_call(
+        functools.partial(merge_kernel, rows),
+        out_shape=jax.ShapeDtypeStruct(got.shape, got.dtype),
+        in_specs=[vmem] * 2,
+        out_specs=vmem,
+        compiler_params=pltpu.CompilerParams(vmem_limit_bytes=16 * 2**20),
+        cost_estimate=pl.CostEstimate(flops=rows * 1024, bytes_accessed=2**19, transcendentals=0),
+    )(own, got)
 
 
 def attend_call(shift, tokens, heads, chips, info, block, priors, pieces, kind):
@@ -356,7 +374,8 @@
     far_part = attend(4, far, (), near, f32)
     far_part = moved(attend(4, far, (far_part,), pieces, bf16), -2)
     back_part = moved(attend(-2, back, (back_part,), pieces, bf16), 2)
-    ahead_part = moved(attend(2, ahead, (ahead_part, far_part), pieces, bf16), -2)
+    ahead_part = attend(2, ahead, (ahead_part,), pieces, f32)
+    ahead_part = moved(merge_call(rows, ahead_part, far_part), -2)
     own = attend(0, queries, (own,), pieces, f32)
     parts = (ahead_part, back_part)
     return pl.pallas_call(

time: 58.4 us -> 60.2 us (1.031)
  the two profiles are of different devices: /device:TPU:2 before, /device:TPU:74 now
where the time goes in v2:
time: 60.2 us
  Pallas kernels  28.5 us (47%)
  starting transfers between devices  17.3 us (29%)
  waiting for transfers between devices  12.9 us (21%)
  other arithmetic  1.38 us (2%)
    pallas_call x8, Pallas kernels, attend_call(): pl.pallas_call(functools.partial(attend_kernel, shift, tokens, heads, chi...  26.8 us
    ppermute x7, starting transfers between devices, moved(): return lax.ppermute(array, 'ctx', pairs)  16.6 us
    ppermute x7, waiting for transfers between devices, moved(): return lax.ppermute(array, 'ctx', pairs)  12.8 us
    concatenate x1, other arithmetic, on_device(): jnp.concatenate([history_keys, new_keys, history_values, fresh_values], a...  1.3 us
    pallas_call x1, Pallas kernels, on_device(): pl.pallas_call(functools.partial(finish_kernel, rows, tokens, heads), out...  1.25 us
  transfers between devices with their start and end apart: 9, of which 4 were waited for; matrix products, arithmetic and copies ran while one was open for 2% of the time, Pallas kernels for 40%

profile of v2, /device:TPU:74, one launch (start us, length us, event | category | flops | bytes accessed | tf_op | source)
XLA Modules:
  0.0 60.2 jit_solution(18359957663029286424)
XLA Ops:
  0.0 0.0 copy-start
  0.0 0.0 copy-start.2
  0.0 0.0 copy-start.1
  0.0 4.6 %collective-permute-start = (bf16[32,2048]{1,0:T(8,128)(2,1)}, bf16[32,2048]{1,0:T(8,128)(2,1)S(1)}, u32[]{:S(2)}, u32[]{:S(2)}) collective-permute-start(bf16[32,2048]{1,0:T(8,128)(2,1)} %q_ref.3), channel_id=1, source_target_pairs={{0,32},{8,104},{16,48},{24,120},{32,64},{40,8},{48,80},{56,24},{64... | collective-permute-start | bytes 393224 | tf_op jit(solution)/shard_map/ppermute | solution.py:355
  4.6 1.3 %pad_maximum_fusion.refs_0_.refs_1_ = bf16[4160,128]{1,0:T(8,128)(2,1)S(1)} fusion(bf16[32,128]{1,0:T(8,128)(2,1)} %param.9, bf16[2048,128]{1,0:T(8,128)(2,1)} %param.11, bf16[32,128]{1,0:T(8,128)(2,1)} %param.8, bf16[2048,128]{1,0:T(8,128)(2,1)} %param.10), kind=kLoop, calls=%fused_computation | loop fusion | flops 4259840 | bytes 2129920 | tf_op jit(solution)/shard_map/concatenate | solution.py:357
  5.9 2.2 %collective-permute-done.q_ref = bf16[32,2048]{1,0:T(8,128)(2,1)S(1)} collective-permute-done((bf16[32,2048]{1,0:T(8,128)(2,1)}, bf16[32,2048]{1,0:T(8,128)(2,1)S(1)}, u32[]{:S(2)}, u32[]{:S(2)}) %collective-permute-start) | collective-permute-done | bytes 131104 | tf_op jit(solution)/shard_map/ppermute | solution.py:355
  8.1 0.0 collective-permute-start.2
  8.1 1.0 %collective-permute-start.1 = (bf16[4160,128]{1,0:T(8,128)(2,1)S(1)}, bf16[4160,128]{1,0:T(8,128)(2,1)S(1)}, u32[]{:S(2)}, u32[]{:S(2)}) collective-permute-start(bf16[4160,128]{1,0:T(8,128)(2,1)S(1)} %pad_maximum_fusion.refs_0_.refs_1_), channel_id=1, source_target_pairs={{0,16},{8,120},{16,32},{24,8},{32,48},{40,24},{48,64},{56,40},{64,... | collective-permute-start | bytes 3194888 | tf_op jit(solution)/shard_map/ppermute | solution.py:355
  9.1 0.0 copy-done
  9.1 2.5 %collective-permute-start.3 = (bf16[32,2048]{1,0:T(8,128)(2,1)S(1)}, bf16[32,2048]{1,0:T(8,128)(2,1)}, u32[]{:S(2)}, u32[]{:S(2)}) collective-permute-start(bf16[32,2048]{1,0:T(8,128)(2,1)S(1)} %copy-done), channel_id=1, source_target_pairs={{0,96},{8,40},{16,112},{24,56},{32,0},{40,72},{48,16},{56,88},{64,... | collective-permute-start | bytes 393224 | tf_op jit(solution)/shard_map/ppermute | solution.py:355
  11.6 0.0 copy-done.2
  11.6 0.0 copy-done.1
  11.6 0.1 pad_add_fusion.info_ref
  11.7 2.7 %collective-permute-start.4 = (bf16[32,2048]{1,0:T(8,128)(2,1)S(1)}, bf16[32,2048]{1,0:T(8,128)(2,1)S(1)}, u32[]{:S(2)}, u32[]{:S(2)}) collective-permute-start(bf16[32,2048]{1,0:T(8,128)(2,1)S(1)} %collective-permute-done.q_ref), channel_id=1, source_target_pairs={{0,32},{8,104},{16,48},{24,120},{32,64},{40,8},{48,80},{56,24},{64... | collective-permute-start | bytes 393224 | tf_op jit(solution)/shard_map/ppermute | solution.py:355
  14.4 0.0 collective-permute-done.2.refs_1_.refs_2_
  14.4 2.1 %shard_map.74.refs_0_ = f32[528,128]{1,0:T(8,128)S(1)} custom-call(s32[10]{0:T(128)S(1)} %pad_add_fusion.info_ref, bf16[32,2048]{1,0:T(8,128)(2,1)S(1)} %collective-permute-done.q_ref, bf16[4160,128]{1,0:T(8,128)(2,1)S(1)} %pad_maximum_fusion.refs_0_.refs_1_, bf16[4160,128]{1,0:T(8,128)(2,1)S(1)} %collective-permute-done.2.refs_1_.refs_2_), custom_call_target="tpu_custom_call" | custom-call | flops 1073741824 | bytes 2097152 | tf_op jit(solution)/shard_map/pallas_call | solution.py:321
  16.5 2.1 %shard_map.73.refs_0_ = f32[528,128]{1,0:T(8,128)S(1)} custom-call(s32[10]{0:T(128)S(1)} %pad_add_fusion.info_ref, bf16[32,2048]{1,0:T(8,128)(2,1)S(1)} %copy-done, bf16[4160,128]{1,0:T(8,128)(2,1)S(1)} %pad_maximum_fusion.refs_0_.refs_1_, bf16[4160,128]{1,0:T(8,128)(2,1)S(1)} %collective-permute-done.2.refs_1_.refs_2_), custom_call_target="tpu_custom_call" | custom-call | flops 1073741824 | bytes 2097152 | tf_op jit(solution)/shard_map/pallas_call | solution.py:321
  18.7 0.3 collective-permute-done.3.q_ref
  19.0 4.6 %shard_map.75.refs_0_ = f32[528,128]{1,0:T(8,128)S(1)} custom-call(s32[10]{0:T(128)S(1)} %pad_add_fusion.info_ref, bf16[32,2048]{1,0:T(8,128)(2,1)} %collective-permute-done.3.q_ref, bf16[4160,128]{1,0:T(8,128)(2,1)S(1)} %pad_maximum_fusion.refs_0_.refs_1_, bf16[4160,128]{1,0:T(8,128)(2,1)S(1)} %collective-permute-done.2.refs_1_.refs_2_), custom_call_target="tpu_custom_call" | custom-call | flops 1073741824 | bytes 2097152 | tf_op jit(solution)/shard_map/pallas_call | solution.py:321
  23.5 6.7 %collective-permute-done.4.q_ref = bf16[32,2048]{1,0:T(8,128)(2,1)S(1)} collective-permute-done((bf16[32,2048]{1,0:T(8,128)(2,1)S(1)}, bf16[32,2048]{1,0:T(8,128)(2,1)S(1)}, u32[]{:S(2)}, u32[]{:S(2)}) %collective-permute-start.4) | collective-permute-done | bytes 131104 | tf_op jit(solution)/shard_map/ppermute | solution.py:355
  30.2 0.0 collective-permute-done.1.refs_3_
  30.2 0.7 %collective-permute-start.5 = (bf16[4160,128]{1,0:T(8,128)(2,1)S(1)}, bf16[4160,128]{1,0:T(8,128)(2,1)S(1)}, u32[]{:S(2)}, u32[]{:S(2)}) collective-permute-start(bf16[4160,128]{1,0:T(8,128)(2,1)S(1)} %collective-permute-done.1.refs_3_), channel_id=1, source_target_pairs={{0,8},{8,0},{16,24},{24,16},{32,40},{40,32},{48,56},{56,48},{64,72... | collective-permute-start | bytes 3194888 | tf_op jit(solution)/shard_map/ppermute | solution.py:351
  30.9 4.2 %shard_map.78.refs_0_ = f32[528,128]{1,0:T(8,128)S(1)} custom-call(s32[10]{0:T(128)S(1)} %pad_add_fusion.info_ref, bf16[32,2048]{1,0:T(8,128)(2,1)S(1)} %collective-permute-done.4.q_ref, bf16[4160,128]{1,0:T(8,128)(2,1)S(1)} %pad_maximum_fusion.refs_0_.refs_1_, bf16[4160,128]{1,0:T(8,128)(2,1)S(1)} %collective-permute-done.2.refs_1_.refs_2_), custom_call_target="tpu_custom_call" | custom-call | flops 1073741824 | bytes 2097152 | tf_op jit(solution)/shard_map/pallas_call | solution.py:321
  35.0 0.0 collective-permute-done.5.refs_4_
  35.1 3.4 %shard_map.79 = bf16[528,128]{1,0:T(8,128)(2,1)S(1)} custom-call(s32[10]{0:T(128)S(1)} %pad_add_fusion.info_ref, bf16[32,2048]{1,0:T(8,128)(2,1)S(1)} %collective-permute-done.4.q_ref, f32[528,128]{1,0:T(8,128)S(1)} %shard_map.78.refs_0_, bf16[4160,128]{1,0:T(8,128)(2,1)S(1)} %pad_maximum_fusion.refs_0_.refs_1_, ...), custom_call_target="tpu_custom_call" | custom-call | flops 1073741824 | bytes 2097152 | tf_op jit(solution)/shard_map/pallas_call | solution.py:321
  38.5 0.1 collective-permute-start.6
  38.6 3.8 %shard_map.81 = bf16[528,128]{1,0:T(8,128)(2,1)S(1)} custom-call(s32[10]{0:T(128)S(1)} %pad_add_fusion.info_ref, bf16[32,2048]{1,0:T(8,128)(2,1)} %collective-permute-done.3.q_ref, f32[528,128]{1,0:T(8,128)S(1)} %shard_map.75.refs_0_, bf16[4160,128]{1,0:T(8,128)(2,1)S(1)} %pad_maximum_fusion.refs_0_.refs_1_, ...), custom_call_target="tpu_custom_call" | custom-call | flops 1073741824 | bytes 2097152 | tf_op jit(solution)/shard_map/pallas_call | solution.py:321
  42.4 5.7 %collective-permute-start.8 = (bf16[528,128]{1,0:T(8,128)(2,1)S(1)}, bf16[528,128]{1,0:T(8,128)(2,1)S(1)}, u32[]{:S(2)}, u32[]{:S(2)}) collective-permute-start(bf16[528,128]{1,0:T(8,128)(2,1)S(1)} %shard_map.81), channel_id=1, source_target_pairs={{0,32},{8,104},{16,48},{24,120},{32,64},{40,8},{48,80},{56,24},{64... | collective-permute-start | bytes 405512 | tf_op jit(solution)/shard_map/ppermute | solution.py:355
  48.1 3.1 %shard_map.77.own_ref = f32[528,128]{1,0:T(8,128)S(1)} custom-call(s32[10]{0:T(128)S(1)} %pad_add_fusion.info_ref, bf16[32,2048]{1,0:T(8,128)(2,1)S(1)} %collective-permute-done.q_ref, f32[528,128]{1,0:T(8,128)S(1)} %shard_map.74.refs_0_, bf16[4160,128]{1,0:T(8,128)(2,1)S(1)} %pad_maximum_fusion.refs_0_.refs_1_, ...), custom_call_target="tpu_custom_call" | custom-call | flops 1073741824 | bytes 2097152 | tf_op jit(solution)/shard_map/pallas_call | solution.py:321
  51.3 0.0 collective-permute-done.6.got_ref
  51.3 0.5 shard_map.80
  51.8 0.1 collective-permute-start.7
  51.9 3.4 %shard_map.76.refs_0_ = f32[528,128]{1,0:T(8,128)S(1)} custom-call(s32[10]{0:T(128)S(1)} %pad_add_fusion.info_ref, bf16[32,2048]{1,0:T(8,128)(2,1)S(1)} %copy-done, f32[528,128]{1,0:T(8,128)S(1)} %shard_map.73.refs_0_, bf16[4160,128]{1,0:T(8,128)(2,1)S(1)} %pad_maximum_fusion.refs_0_.refs_1_, bf16[4160,128]{1,0:T(8,128)(2,1)S(1)} %collective-permute-done.2.refs_1_.refs_2_, ...), custom_call_target="tpu_custom_call" | custom-call | flops 1073741824 | bytes 2097152 | tf_op jit(solution)/shard_map/pallas_call | solution.py:321
  55.3 0.0 collective-permute-done.8.refs_2_
  55.3 3.6 %collective-permute-done.7.refs_1_ = bf16[528,128]{1,0:T(8,128)(2,1)S(1)} collective-permute-done((bf16[528,128]{1,0:T(8,128)(2,1)S(1)}, bf16[528,128]{1,0:T(8,128)(2,1)S(1)}, u32[]{:S(2)}, u32[]{:S(2)}) %collective-permute-start.7) | collective-permute-done | bytes 135200 | tf_op jit(solution)/shard_map/ppermute | solution.py:355
  59.0 1.3 %shard_map.82 = bf16[32,2048]{1,0:T(8,128)(2,1)} custom-call(f32[528,128]{1,0:T(8,128)S(1)} %shard_map.76.refs_0_, bf16[528,128]{1,0:T(8,128)(2,1)S(1)} %collective-permute-done.7.refs_1_, bf16[528,128]{1,0:T(8,128)(2,1)S(1)} %collective-permute-done.8.refs_2_), custom_call_target="tpu_custom_call" | custom-call | flops 1048576 | bytes 524288 | tf_op jit(solution)/shard_map/pallas_call | solution.py:381
Async XLA Ops:
  0.0 9.1 %copy-start = (bf16[32,2048]{1,0:T(8,128)(2,1)S(1)}, bf16[32,2048]{1,0:T(8,128)(2,1)}, u32[]{:S(2)}) copy-start(bf16[32,2048]{1,0:T(8,128)(2,1)} %q_ref.3) | copy-start | bytes 393220
  0.0 11.6 %copy-start.2 = (s32[4]{0:T(128)S(1)}, s32[4]{0:T(128)}, u32[]{:S(2)}) copy-start(s32[4]{0:T(128)} %param.12) | copy-start | bytes 52
  0.0 11.6 %copy-start.1 = (s32[4]{0:T(128)S(1)}, s32[4]{0:T(128)}, u32[]{:S(2)}) copy-start(s32[4]{0:T(128)} %param.13) | copy-start | bytes 52
  0.0 8.1 %collective-permute-start = (bf16[32,2048]{1,0:T(8,128)(2,1)}, bf16[32,2048]{1,0:T(8,128)(2,1)S(1)}, u32[]{:S(2)}, u32[]{:S(2)}) collective-permute-start(bf16[32,2048]{1,0:T(8,128)(2,1)} %q_ref.3), channel_id=1, source_target_pairs={{0,32},{8,104},{16,48},{24,120},{32,64},{40,8},{48,80},{56,24},{64... | collective-permute-start | bytes 393224 | tf_op jit(solution)/shard_map/ppermute | solution.py:355
  8.1 6.3 %collective-permute-start.2 = (bf16[4160,128]{1,0:T(8,128)(2,1)S(1)}, bf16[4160,128]{1,0:T(8,128)(2,1)S(1)}, u32[]{:S(2)}, u32[]{:S(2)}) collective-permute-start(bf16[4160,128]{1,0:T(8,128)(2,1)S(1)} %pad_maximum_fusion.refs_0_.refs_1_), channel_id=1, source_target_pairs={{0,8},{8,0},{16,24},{24,16},{32,40},{40,32},{48,56},{56,48},{64,72... | collective-permute-start | bytes 3194888 | tf_op jit(solution)/shard_map/ppermute | solution.py:351
  8.1 22.1 %collective-permute-start.1 = (bf16[4160,128]{1,0:T(8,128)(2,1)S(1)}, bf16[4160,128]{1,0:T(8,128)(2,1)S(1)}, u32[]{:S(2)}, u32[]{:S(2)}) collective-permute-start(bf16[4160,128]{1,0:T(8,128)(2,1)S(1)} %pad_maximum_fusion.refs_0_.refs_1_), channel_id=1, source_target_pairs={{0,16},{8,120},{16,32},{24,8},{32,48},{40,24},{48,64},{56,40},{64,... | collective-permute-start | bytes 3194888 | tf_op jit(solution)/shard_map/ppermute | solution.py:355
  9.1 9.9 %collective-permute-start.3 = (bf16[32,2048]{1,0:T(8,128)(2,1)S(1)}, bf16[32,2048]{1,0:T(8,128)(2,1)}, u32[]{:S(2)}, u32[]{:S(2)}) collective-permute-start(bf16[32,2048]{1,0:T(8,128)(2,1)S(1)} %copy-done), channel_id=1, source_target_pairs={{0,96},{8,40},{16,112},{24,56},{32,0},{40,72},{48,16},{56,88},{64,... | collective-permute-start | bytes 393224 | tf_op jit(solution)/shard_map/ppermute | solution.py:355
  11.7 18.5 %collective-permute-start.4 = (bf16[32,2048]{1,0:T(8,128)(2,1)S(1)}, bf16[32,2048]{1,0:T(8,128)(2,1)S(1)}, u32[]{:S(2)}, u32[]{:S(2)}) collective-permute-start(bf16[32,2048]{1,0:T(8,128)(2,1)S(1)} %collective-permute-done.q_ref), channel_id=1, source_target_pairs={{0,32},{8,104},{16,48},{24,120},{32,64},{40,8},{48,80},{56,24},{64... | collective-permute-start | bytes 393224 | tf_op jit(solution)/shard_map/ppermute | solution.py:355
  30.2 4.9 %collective-permute-start.5 = (bf16[4160,128]{1,0:T(8,128)(2,1)S(1)}, bf16[4160,128]{1,0:T(8,128)(2,1)S(1)}, u32[]{:S(2)}, u32[]{:S(2)}) collective-permute-start(bf16[4160,128]{1,0:T(8,128)(2,1)S(1)} %collective-permute-done.1.refs_3_), channel_id=1, source_target_pairs={{0,8},{8,0},{16,24},{24,16},{32,40},{40,32},{48,56},{56,48},{64,72... | collective-permute-start | bytes 3194888 | tf_op jit(solution)/shard_map/ppermute | solution.py:351
  38.5 12.8 %collective-permute-start.6 = (bf16[528,128]{1,0:T(8,128)(2,1)S(1)}, bf16[528,128]{1,0:T(8,128)(2,1)S(1)}, u32[]{:S(2)}, u32[]{:S(2)}) collective-permute-start(bf16[528,128]{1,0:T(8,128)(2,1)S(1)} %shard_map.79), channel_id=1, source_target_pairs={{0,96},{8,40},{16,112},{24,56},{32,0},{40,72},{48,16},{56,88},{64,... | collective-permute-start | bytes 405512 | tf_op jit(solution)/shard_map/ppermute | solution.py:355
  42.4 12.9 %collective-permute-start.8 = (bf16[528,128]{1,0:T(8,128)(2,1)S(1)}, bf16[528,128]{1,0:T(8,128)(2,1)S(1)}, u32[]{:S(2)}, u32[]{:S(2)}) collective-permute-start(bf16[528,128]{1,0:T(8,128)(2,1)S(1)} %shard_map.81), channel_id=1, source_target_pairs={{0,32},{8,104},{16,48},{24,120},{32,64},{40,8},{48,80},{56,24},{64... | collective-permute-start | bytes 405512 | tf_op jit(solution)/shard_map/ppermute | solution.py:355
  51.8 7.2 %collective-permute-start.7 = (bf16[528,128]{1,0:T(8,128)(2,1)S(1)}, bf16[528,128]{1,0:T(8,128)(2,1)S(1)}, u32[]{:S(2)}, u32[]{:S(2)}) collective-permute-start(bf16[528,128]{1,0:T(8,128)(2,1)S(1)} %shard_map.80), channel_id=1, source_target_pairs={{0,96},{8,40},{16,112},{24,56},{32,0},{40,72},{48,16},{56,88},{64,... | collective-permute-start | bytes 405512 | tf_op jit(solution)/shard_map/ppermute | solution.py:355
